TPU v7x, 512 devices: a whole 4x8x8 slice. The times are simulated.
512 devices in a mesh: wide: 128 (over z, y, core), narrow: 4 (over x).
Axes of the slice: x: 4, y: 8, z: 8, core: 2. Of those that a mesh axis runs over, the one named last changes fastest.
Arguments:
- slab: bfloat16 [98304, 2048], P('wide', 'narrow'), may hold values from -1.1953125 to 1.1953125
- occupation: float32 [4096], replicated, may hold values from 0.02 to 2
- column_band: int32 [2048], P('narrow'), may hold values from 0 to 4095
- pattern: int32 [768, 12], P('wide'), may hold values from 0 to 767, as said below
Outputs:
- density: bfloat16 [768, 12, 128, 128], P('wide', 'narrow')
Inputs may be any that keep to these rules, and one draw needn't show every extreme that they name: `pattern`: each row c lists 12 different clusters, each equal to (c + d) mod 768 with -8 <= d <= 8; d = -8 and d = 8 appear in every row.
All inputs are finite; a program needn't handle non-finite values.
Results may differ from a plain program's by a relative error of at most 0.015.
Values may be sent and summed in bfloat16 or wider, within the bound.
A program may use at most 64 MiB of HBM per device.

v0:
```python
import jax
import jax.numpy as jnp
from jax import lax
from jax.sharding import PartitionSpec as P

B = 128
REACH = 8


def from_behind(value, axis, steps):
    count = lax.axis_size(axis)
    pairs = [(source, (source + steps) % count) for source in range(count)]
    return lax.ppermute(value, axis, pairs)


def fetch_rows(slab, steps):
    return from_behind(slab, "wide", steps)


def per_device(slab, occupation, column_band, pattern):
    cl_dev = slab.shape[0] // B
    local_cols = slab.shape[1]
    hops = -(-REACH // cl_dev)
    clusters = cl_dev * lax.axis_size("wide")
    picks = column_band[:, None] == jnp.arange(occupation.shape[0], dtype=jnp.int32)[None, :]
    weight = jnp.sum(jnp.where(picks, occupation[None, :], jnp.float32(0.0)), axis=1)
    scaled = (slab.astype(jnp.float32) * weight[None, :]).astype(jnp.bfloat16)
    pieces = []
    for steps in range(hops, 0, -1):
        pieces.append(fetch_rows(slab, steps))
    pieces.append(slab)
    for steps in range(1, hops + 1):
        pieces.append(fetch_rows(slab, -steps))
    window = jnp.concatenate(pieces, axis=0).reshape(-1, B, local_cols)
    first = lax.axis_index("wide") * cl_dev - hops * cl_dev
    local_index = jnp.mod(pattern - first, clusters)
    right = jnp.take(window, local_index.reshape(-1), axis=0).reshape(
        cl_dev, pattern.shape[1], B, local_cols
    )
    left = scaled.reshape(cl_dev, B, local_cols)
    partial_blocks = jnp.einsum("rik,rnjk->rnij", left, right, preferred_element_type=jnp.float32)
    summed = lax.psum(partial_blocks.astype(jnp.bfloat16), "narrow").astype(jnp.float32)
    share = pattern.shape[1] // lax.axis_size("narrow")
    start = lax.axis_index("narrow") * share
    mine = lax.dynamic_slice_in_dim(summed, start, share, 1)
    return mine.astype(jnp.bfloat16)


def solution(mesh):
    placed = (P("wide", "narrow"), P(), P("narrow"), P("wide", None))
    return jax.shard_map(
        per_device,
        mesh=mesh,
        in_specs=placed,
        out_specs=P("wide", "narrow", None, None),
        check_vma=False,
    )
```

profile of v0, /device:TPU:1, one launch (start us, length us, event | category | flops | bytes accessed | tf_op | source)
XLA Modules:
  0.0 148.8 jit_solution(14234777423950304499)
XLA Ops:
  6.5 0.0 copy-start
  6.5 0.0 all-reduce.2.cloned.1.call-start
  6.5 4.2 %collective-permute-start = (bf16[768,512]{1,0:T(8,128)(2,1)}, bf16[768,512]{1,0:T(8,128)(2,1)}, u32[]{:S(2)}, u32[]{:S(2)}) collective-permute-start(bf16[768,512]{1,0:T(8,128)(2,1)} %param.4), channel_id=1, source_target_pairs={{0,8},{4,12},{8,16},{12,20},{16,24},{20,28},{24,32},{28,36},{32,40... | collective-permute-start | bytes 2359304 | tf_op jit(solution)/shard_map/ppermute | solution.py:13
  10.7 4.0 %collective-permute-start.1 = (bf16[768,512]{1,0:T(8,128)(2,1)}, bf16[768,512]{1,0:T(8,128)(2,1)S(1)}, u32[]{:S(2)}, u32[]{:S(2)}) collective-permute-start(bf16[768,512]{1,0:T(8,128)(2,1)} %param.4), channel_id=1, source_target_pairs={{0,4},{4,8},{8,12},{12,16},{16,20},{20,24},{24,28},{28,32},{32,36}... | collective-permute-start | bytes 2359304 | tf_op jit(solution)/shard_map/ppermute | solution.py:13
  14.8 4.6 %collective-permute-start.2 = (bf16[768,512]{1,0:T(8,128)(2,1)}, bf16[768,512]{1,0:T(8,128)(2,1)S(1)}, u32[]{:S(2)}, u32[]{:S(2)}) collective-permute-start(bf16[768,512]{1,0:T(8,128)(2,1)} %param.4), channel_id=1, source_target_pairs={{0,508},{4,0},{8,4},{12,8},{16,12},{20,16},{24,20},{28,24},{32,28}... | collective-permute-start | bytes 2359304 | tf_op jit(solution)/shard_map/ppermute | solution.py:13
  19.3 8.2 %collective-permute-start.3 = (bf16[768,512]{1,0:T(8,128)(2,1)}, bf16[768,512]{1,0:T(8,128)(2,1)S(1)}, u32[]{:S(2)}, u32[]{:S(2)}) collective-permute-start(bf16[768,512]{1,0:T(8,128)(2,1)} %param.4), channel_id=1, source_target_pairs={{0,504},{4,508},{8,0},{12,4},{16,8},{20,12},{24,16},{28,20},{32,24... | collective-permute-start | bytes 2359304 | tf_op jit(solution)/shard_map/ppermute | solution.py:13
  27.5 1.9 %select_reduce_fusion = f32[512]{0:T(512)S(1)} fusion(f32[4096]{0:T(1024)} %param.5, s32[512]{0:T(512)} %param.6), kind=kLoop, calls=%fused_computation.4 | loop fusion | flops 6290944 | bytes 20480 | tf_op jit(solution)/shard_map/reduce_sum | solution.py:26
  29.5 0.7 compare_and_fusion
  30.2 0.1 reshape.50
  30.3 2.2 %multiply_convert_fusion = bf16[768,512]{1,0:T(8,128)(2,1)} fusion(bf16[768,512]{1,0:T(8,128)(2,1)} %param.4, f32[512]{0:T(512)S(1)} %select_reduce_fusion), kind=kLoop, calls=%fused_computation.8 | loop fusion | flops 1179648 | bytes 1574912 | tf_op jit(solution)/shard_map/convert_element_type | solution.py:27
  32.4 6.2 %collective-permute-done = bf16[768,512]{1,0:T(8,128)(2,1)} collective-permute-done((bf16[768,512]{1,0:T(8,128)(2,1)}, bf16[768,512]{1,0:T(8,128)(2,1)}, u32[]{:S(2)}, u32[]{:S(2)}) %collective-permute-start) | collective-permute-done | bytes 786464 | tf_op jit(solution)/shard_map/ppermute | solution.py:13
  38.6 2.1 %constant_dynamic-update-slice_fusion.4 = bf16[3840,512]{1,0:T(8,128)(2,1)} fusion(bf16[768,512]{1,0:T(8,128)(2,1)} %collective-permute-done), kind=kLoop, calls=%fused_computation.15 | loop fusion | bytes 1572864
  40.7 0.0 collective-permute-done.1
  40.7 0.9 constant_dynamic-update-slice_fusion.3
  41.6 0.0 copy-done
  41.7 0.9 constant_dynamic-update-slice_fusion.2
  42.6 0.0 collective-permute-done.2
  42.6 0.9 constant_dynamic-update-slice_fusion.1
  43.5 1.7 %collective-permute-done.3 = bf16[768,512]{1,0:T(8,128)(2,1)S(1)} collective-permute-done((bf16[768,512]{1,0:T(8,128)(2,1)}, bf16[768,512]{1,0:T(8,128)(2,1)S(1)}, u32[]{:S(2)}, u32[]{:S(2)}) %collective-permute-start.3) | collective-permute-done | bytes 786464 | tf_op jit(solution)/shard_map/ppermute | solution.py:13
  45.2 1.0 constant_dynamic-update-slice_fusion
  46.2 0.0 copy-start.1
  46.2 8.1 %gather_fusion = bf16[72,128,512]{2,1,0:T(8,128)(2,1)} fusion(bf16[30,128,512]{2,1,0:T(8,128)(2,1)} %bitcast, s32[1024]{0:T(1024)S(1)} %pad_clamp_fusion), kind=kCustom, calls=%fused_computation | custom fusion | bytes 18874656 | tf_op jit(solution)/shard_map/jit(_take)/gather | solution.py:37
  54.3 0.0 copy-done.1
  54.3 7.7 %convert_bitcast_fusion = bf16[6,12,128,128]{2,3,1,0:T(8,128)(2,1)} fusion(bf16[6,128,512,1]{2,1,3,0:T(8,128)(2,1)S(1)} %bitcast.13, bf16[6,12,128,512]{3,2,1,0:T(8,128)(2,1)} %bitcast.12, pred[6,12]{1,0:T(8,128)(4,1)S(1)} %get-tuple-element.5), kind=kOutput, calls=%fused_computation.7 | convolution fusion | flops 1213857792 | bytes 12582984 | tf_op jit(solution)/shard_map/rik,rnjk->rnij/dot_general | solution.py:41
  62.1 0.0 all-reduce.2.cloned.1.call-update
  62.1 77.7 %all-reduce.2.cloned.1.call-done = bf16[6,12,128,128]{2,3,1,0:T(8,128)(2,1)} async-done(((bf16[6,12,128,128]{2,3,1,0:T(8,128)(2,1)}), bf16[6,12,128,128]{2,3,1,0:T(8,128)(2,1)}) %all-reduce.2.cloned.1.call-update) | async-done | bytes 2359312 | tf_op jit(solution)/shard_map/psum | solution.py:42
  139.8 1.1 convert_convert_fusion
  140.9 1.1 copy.6
  (2 shorter events, 0.0 us)
Async XLA Ops:
  6.5 35.1 %copy-start = (bf16[768,512]{1,0:T(8,128)(2,1)S(1)}, bf16[768,512]{1,0:T(8,128)(2,1)}, u32[]{:S(2)}) copy-start(bf16[768,512]{1,0:T(8,128)(2,1)} %param.4) | copy-start | bytes 2359300
  6.5 133.2 %all-reduce.2.cloned.1.call-start = ((), (), s32[]{:S(2)}) async-start(), calls=%async_computation | async-start | bytes 4718592 | tf_op jit(solution)/shard_map/psum | solution.py:42
  6.5 32.1 %collective-permute-start = (bf16[768,512]{1,0:T(8,128)(2,1)}, bf16[768,512]{1,0:T(8,128)(2,1)}, u32[]{:S(2)}, u32[]{:S(2)}) collective-permute-start(bf16[768,512]{1,0:T(8,128)(2,1)} %param.4), channel_id=1, source_target_pairs={{0,8},{4,12},{8,16},{12,20},{16,24},{20,28},{24,32},{28,36},{32,40... | collective-permute-start | bytes 2359304 | tf_op jit(solution)/shard_map/ppermute | solution.py:13
  10.7 30.0 %collective-permute-start.1 = (bf16[768,512]{1,0:T(8,128)(2,1)}, bf16[768,512]{1,0:T(8,128)(2,1)S(1)}, u32[]{:S(2)}, u32[]{:S(2)}) collective-permute-start(bf16[768,512]{1,0:T(8,128)(2,1)} %param.4), channel_id=1, source_target_pairs={{0,4},{4,8},{8,12},{12,16},{16,20},{20,24},{24,28},{28,32},{32,36}... | collective-permute-start | bytes 2359304 | tf_op jit(solution)/shard_map/ppermute | solution.py:13
  14.8 27.8 %collective-permute-start.2 = (bf16[768,512]{1,0:T(8,128)(2,1)}, bf16[768,512]{1,0:T(8,128)(2,1)S(1)}, u32[]{:S(2)}, u32[]{:S(2)}) collective-permute-start(bf16[768,512]{1,0:T(8,128)(2,1)} %param.4), channel_id=1, source_target_pairs={{0,508},{4,0},{8,4},{12,8},{16,12},{20,16},{24,20},{28,24},{32,28}... | collective-permute-start | bytes 2359304 | tf_op jit(solution)/shard_map/ppermute | solution.py:13
  19.3 25.9 %collective-permute-start.3 = (bf16[768,512]{1,0:T(8,128)(2,1)}, bf16[768,512]{1,0:T(8,128)(2,1)S(1)}, u32[]{:S(2)}, u32[]{:S(2)}) collective-permute-start(bf16[768,512]{1,0:T(8,128)(2,1)} %param.4), channel_id=1, source_target_pairs={{0,504},{4,508},{8,0},{12,4},{16,8},{20,12},{24,16},{28,20},{32,24... | collective-permute-start | bytes 2359304 | tf_op jit(solution)/shard_map/ppermute | solution.py:13
  46.2 8.1 %copy-start.1 = (bf16[768,512]{1,0:T(8,128)(2,1)S(1)}, bf16[768,512]{1,0:T(8,128)(2,1)}, u32[]{:S(2)}) copy-start(bf16[768,512]{1,0:T(8,128)(2,1)} %multiply_convert_fusion) | copy-start | bytes 2359300
Sparse Core Ops, SparseCore 0:
  62.2 77.5 all-reduce.1
where the time goes:
time: 149 us
  waiting for transfers between devices  85.6 us (57%)
  starting transfers between devices  21 us (14%)
  local copies, waits for them, and re-layouts  15.1 us (10%)
  between operations  13.4 us (9%)
  matrix products  7.73 us (5%)
  other arithmetic  5.92 us (4%)
    psum x1, waiting for transfers between devices, per_device(): lax.psum(partial_blocks.astype(jnp.bfloat16), 'narrow').astype(jnp.float32)  77.7 us
    ppermute x4, starting transfers between devices, from_behind(): return lax.ppermute(value, axis, pairs)  21 us
    gather x1, local copies, waits for them, and re-layouts, per_device(): jnp.take(window, local_index.reshape(-1), axis=0)  8.11 us
    ppermute x4, waiting for transfers between devices, from_behind(): return lax.ppermute(value, axis, pairs)  7.92 us
    dot_general x1, matrix products, per_device(): jnp.einsum('rik,rnjk->rnij', left, right, preferred_element_type=jnp.floa...  7.73 us
    unnamed x8, local copies, waits for them, and re-layouts  4.9 us
  transfers between devices with their start and end apart: 5, of which 3 were waited for; matrix products, arithmetic and copies ran while one was open for 7% of the time, Pallas kernels for 0%

commit v1 on v0

v1 whole, which is shorter than its diff:
```python
import functools

import jax
import jax.numpy as jnp
from jax import lax
from jax.experimental import pallas as pl
from jax.experimental.pallas import tpu as pltpu
from jax.sharding import PartitionSpec as P

MESH = pl.DeviceIdType.MESH
B = 128
REACH = 8
BAND = 2 * REACH + 1
OWN = 6
WINDOW = OWN + 2 * REACH
NJ = 2
JC = B // NJ
HALF = JC // 2
JOBS = OWN * NJ
SHARE = 3


def kernel(
    n_clusters, slab, occ, band, pattern, out,
    window, scaled, blocks, parts, first_up, first_down, sum_up, sum_down, total, result,
    occ_v, band_v, pat,
    own_sem, in_sem, halo_recv, near_send, core_send, far_send, relay_send,
    up1_send, up1_recv, down1_send, down1_recv, up2_send, up2_recv, down2_send, down2_recv, out_sem,
):
    wide = lax.axis_index("wide")
    here = lax.axis_index("narrow")
    n_chips = lax.axis_size("wide") // 2
    n_narrow = lax.axis_size("narrow")
    chip, core = wide // 2, lax.rem(wide, 2)
    outward = 2 * core - 1
    near_chip = lax.rem(chip + outward + n_chips, n_chips)
    far_chip = lax.rem(chip - outward + n_chips, n_chips)
    other = (chip * 2 + 1 - core, here)
    near_other = (near_chip * 2 + 1 - core, here)
    near_same = (near_chip * 2 + core, here)
    far_same = (far_chip * 2 + core, here)
    up = (wide, lax.rem(here + 1, n_narrow))
    down = (wide, lax.rem(here + n_narrow - 1, n_narrow))

    def cluster(pos):
        return jnp.where(core == 0, pos, OWN - 1 - pos)

    own = [
        pltpu.make_async_copy(slab.at[cluster(p)], window.at[:, REACH + p], own_sem.at[p])
        for p in range(OWN)
    ]
    small = [
        pltpu.make_async_copy(occ, occ_v, in_sem.at[0]),
        pltpu.make_async_copy(band, band_v, in_sem.at[1]),
        pltpu.make_async_copy(pattern, pat, in_sem.at[2]),
    ]
    for copy in own + small:
        copy.start()

    barrier = pltpu.get_barrier_semaphore()
    for device in (other, near_other, near_same, up, down):
        pl.semaphore_signal(barrier, inc=1, device_id=device, device_id_type=MESH)
    pl.semaphore_wait(barrier, 5)

    def remote(src, dst, send_sem, recv_sem, device):
        return pltpu.make_async_remote_copy(
            src_ref=src, dst_ref=dst, send_sem=send_sem, recv_sem=recv_sem,
            device_id=device, device_id_type=MESH,
        )

    def halo(h, src, to, send_sem, device):
        return remote(src, window.at[h, to], send_sem, halo_recv.at[h, to], device)

    def near_copy(h, p):
        return halo(h, slab.at[cluster(p), h], 7 - p, near_send.at[h, p], near_other)

    def core_copy(h, p):
        return halo(h, slab.at[cluster(p), h], 19 - p, core_send.at[h, p], other)

    def far_copy(h, p):
        return halo(h, slab.at[cluster(p), h], p - 4, far_send.at[h, p - 4], far_same)

    def relay_copy(h, k):
        return halo(h, window.at[h, k], 27 - k, relay_send.at[h, 7 - k], other)

    def arrived(h, k):
        halo(h, window.at[h, k], k, relay_send.at[h, 0], other).wait_recv()

    def send_for(job):
        s, h = divmod(job, NJ)
        if s == 0:
            for p in range(3):
                near_copy(h, p).start()
        elif s <= 3:
            near_copy(h, s + 2).start()
        else:
            far_copy(h, 9 - s).start()

    with jax.named_scope("first_sends"):
        send_for(0)
        for h in range(NJ):
            for p in range(OWN):
                core_copy(h, p).start()
        send_for(1)

    with jax.named_scope("weights"):
        for copy in small:
            copy.wait()
        table = occ_v[...]
        turned = jnp.transpose(
            jnp.concatenate([table, jnp.zeros((B - table.shape[0], B), jnp.float32)], axis=0)
        )
        bands = band_v[...]
        high, low = bands // B, lax.rem(bands, B)
        cols = bands.shape[1]
        at = lax.broadcasted_iota(jnp.int32, (B, cols), 0)
        pick_high = jnp.where(at == high, 1.0, 0.0).astype(jnp.bfloat16)
        pick_low = at == low
        rest, looked = turned, jnp.zeros((B, cols), jnp.float32)
        found = []
        for _ in range(3):
            piece = rest.astype(jnp.bfloat16)
            rest = rest - piece.astype(jnp.float32)
            found.append(jnp.dot(piece, pick_high, preferred_element_type=jnp.float32))
        looked = (found[2] + found[1]) + found[0]
        weight = jnp.sum(jnp.where(pick_low, looked, 0.0), axis=0, keepdims=True)

    with jax.named_scope("scale"):
        for p in range(OWN):
            own[p].wait()
            for h in range(NJ):
                rows = window[h, REACH + p].astype(jnp.float32) * weight
                scaled[p, pl.ds(h * JC, JC)] = rows.astype(jnp.bfloat16)

    def up1(job):
        return remote(parts.at[job, 2, 0], first_up.at[job], up1_send.at[job], up1_recv.at[job], up)

    def down1(job):
        return remote(parts.at[job, 2, 1], first_down.at[job], down1_send.at[job], down1_recv.at[job], down)

    def up2(job):
        return remote(parts.at[job, 1], sum_up.at[job], up2_send.at[job], up2_recv.at[job], up)

    def down2(job):
        return remote(parts.at[job, 3], sum_down.at[job], down2_send.at[job], down2_recv.at[job], down)

    def place(job):
        s, h = divmod(job, NJ)
        return OWN - 1 - s, h

    def compute(job):
        p, h = place(job)
        right = window[h, p : p + BAND].reshape(BAND * JC, -1)
        product = lax.dot_general(
            right, scaled[p], (((1,), (1,)), ((), ())), preferred_element_type=jnp.float32
        )
        blocks[...] = product.astype(jnp.bfloat16).reshape(BAND, JC, B)
        c = cluster(p)
        mine = wide * OWN + c
        for r in (2, 1, 3, 0):
            for m in range(SHARE):
                slot = lax.rem(here + r, n_narrow) * SHARE + m
                offset = lax.rem(pat[c, slot] - mine + (REACH + n_clusters), n_clusters)
                offset = jnp.clip(offset, 0, BAND - 1)
                entry = jnp.where(core == 0, offset, BAND - 1 - offset)
                block = blocks[entry]
                parts[job, r, 0, m] = block[:HALF]
                parts[job, r, 1, m] = block[HALF:]
            if r == 2:
                up1(job).start()
                down1(job).start()

    def pass_on(job):
        up1(job).wait_recv()
        parts[job, 1, 0] = (
            parts[job, 1, 0].astype(jnp.float32) + first_up[job].astype(jnp.float32)
        ).astype(jnp.bfloat16)
        up2(job).start()
        down1(job).wait_recv()
        parts[job, 3, 1] = (
            parts[job, 3, 1].astype(jnp.float32) + first_down[job].astype(jnp.float32)
        ).astype(jnp.bfloat16)
        down2(job).start()

    def finish(job):
        p, h = place(job)
        c = cluster(p)
        up2(job).wait_recv()
        down2(job).wait_recv()
        for half in range(2):
            total[:, pl.ds(h * JC + half * HALF, HALF)] = (
                parts[job, 0, half].astype(jnp.float32)
                + sum_up[job, half].astype(jnp.float32)
                + sum_down[job, half].astype(jnp.float32)
            )
        if h == NJ - 1:
            for m in range(SHARE):
                result[c, m] = jnp.transpose(total[m]).astype(jnp.bfloat16)
            pltpu.make_async_copy(result.at[c], out.at[c], out_sem.at[p]).start()

    for job in range(JOBS):
        p, h = place(job)
        with jax.named_scope("wait_halo"):
            if job < NJ:
                for k in (7, 6):
                    arrived(h, k)
                    relay_copy(h, k).start()
                for k in (5, 14, 15, 16, 17, 18, 19, 20, 21):
                    arrived(h, k)
            else:
                arrived(h, p)
        if job + 2 < JOBS:
            send_for(job + 2)
        with jax.named_scope("blocks"):
            compute(job)
        if job >= 1:
            with jax.named_scope("pass_on"):
                pass_on(job - 1)
        if job >= 3:
            with jax.named_scope("finish"):
                finish(job - 3)
    with jax.named_scope("pass_on"):
        pass_on(JOBS - 1)
    with jax.named_scope("finish"):
        for job in range(JOBS - 3, JOBS):
            finish(job)

    with jax.named_scope("drain"):
        for h in range(NJ):
            for p in range(OWN):
                near_copy(h, p).wait_send()
                core_copy(h, p).wait_send()
            for p in (4, 5):
                far_copy(h, p).wait_send()
            for k in (7, 6):
                relay_copy(h, k).wait_send()
        for job in range(JOBS):
            up1(job).wait_send()
            down1(job).wait_send()
            up2(job).wait_send()
            down2(job).wait_send()
        for p in range(OWN):
            c = cluster(p)
            pltpu.make_async_copy(result.at[c], out.at[c], out_sem.at[p]).wait()


def per_device(slab, occupation, column_band, pattern):
    cols = slab.shape[1]
    n_clusters = OWN * lax.axis_size("wide")
    dma = pltpu.SemaphoreType.DMA
    bf16, f32 = jnp.bfloat16, jnp.float32
    return pl.pallas_call(
        functools.partial(kernel, n_clusters),
        out_shape=jax.ShapeDtypeStruct((OWN, SHARE, B, B), bf16),
        in_specs=[pl.BlockSpec(memory_space=pl.ANY)] * 4,
        out_specs=pl.BlockSpec(memory_space=pl.ANY),
        scratch_shapes=[
            pltpu.VMEM((NJ, WINDOW, JC, cols), bf16),
            pltpu.VMEM((OWN, B, cols), bf16),
            pltpu.VMEM((BAND, JC, B), bf16),
            pltpu.VMEM((JOBS, 4, 2, SHARE, HALF, B), bf16),
            pltpu.VMEM((JOBS, SHARE, HALF, B), bf16),
            pltpu.VMEM((JOBS, SHARE, HALF, B), bf16),
            pltpu.VMEM((JOBS, 2, SHARE, HALF, B), bf16),
            pltpu.VMEM((JOBS, 2, SHARE, HALF, B), bf16),
            pltpu.VMEM((SHARE, B, B), f32),
            pltpu.VMEM((OWN, SHARE, B, B), bf16),
            pltpu.VMEM((occupation.shape[0] // B, B), f32),
            pltpu.VMEM((1, cols), jnp.int32),
            pltpu.SMEM(pattern.shape, jnp.int32),
            dma((OWN,)), dma((3,)), dma((NJ, WINDOW)),
            dma((NJ, OWN)), dma((NJ, OWN)), dma((NJ, 2)), dma((NJ, 2)),
            *[dma((JOBS,))] * 8,
            dma((OWN,)),
        ],
        compiler_params=pltpu.CompilerParams(
            collective_id=0, has_side_effects=True, vmem_limit_bytes=40 * 2**20
        ),
        cost_estimate=pl.CostEstimate(
            flops=2 * OWN * BAND * B * B * cols, bytes_accessed=4 * 2**20, transcendentals=0
        ),
        name="density_blocks",
    )(
        slab.reshape(OWN, NJ, JC, cols),
        occupation.reshape(-1, B),
        column_band.reshape(1, -1),
        pattern,
    )


def solution(mesh):
    placed = (P("wide", "narrow"), P(), P("narrow"), P("wide", None))
    return jax.shard_map(
        per_device,
        mesh=mesh,
        in_specs=placed,
        out_specs=P("wide", "narrow", None, None),
        check_vma=False,
    )
```

time: 149 us -> 58.1 us (0.39)
  the two profiles are of different devices: /device:TPU:1 before, /device:TPU:2 now
where the time goes in v1:
time: 58.1 us; the launch traced here: 57.8 us
  Pallas kernels  53.8 us (93%)
  local copies, waits for them, and re-layouts  4.03 us (7%)
    pallas_call x1, Pallas kernels, per_device(): pl.pallas_call(functools.partial(kernel, n_clusters), out_shape=jax.Shape...  53.8 us
    unnamed x9, local copies, waits for them, and re-layouts  4.03 us

profile of v1, /device:TPU:2, one launch (start us, length us, event | category | flops | bytes accessed | tf_op | source)
XLA Modules:
  0.0 57.8 jit_solution(4947653668731047306)
XLA Ops:
  0.0 0.0 copy-start.2
  0.0 0.7 %copy-done.2 = s32[6,12]{1,0:T(8,128)S(1)} copy-done((s32[6,12]{1,0:T(8,128)S(1)}, s32[6,12]{1,0:T(8,128)}, u32[]{:S(2)}) %copy-start.2) | copy-done | bytes 312
  0.7 0.0 copy-start
  0.7 1.1 %copy-done = bf16[768,512]{1,0:T(8,128)(2,1)S(1)} copy-done((bf16[768,512]{1,0:T(8,128)(2,1)S(1)}, bf16[768,512]{1,0:T(8,128)(2,1)}, u32[]{:S(2)}) %copy-start) | copy-done | bytes 786456
  1.8 0.0 copy-start.1
  1.8 0.7 %copy-done.1 = f32[4096]{0:T(1024)S(1)} copy-done((f32[4096]{0:T(1024)S(1)}, f32[4096]{0:T(1024)}, u32[]{:S(2)}) %copy-start.1) | copy-done | bytes 16408
  2.5 0.0 copy-start.3
  2.5 0.7 %copy-done.3 = s32[512]{0:T(512)S(1)} copy-done((s32[512]{0:T(512)S(1)}, s32[512]{0:T(512)}, u32[]{:S(2)}) %copy-start.3) | copy-done | bytes 2072
  3.2 53.8 %density_blocks.1 = bf16[6,3,128,128]{3,2,1,0:T(8,128)(2,1)S(1)} custom-call(bf16[6,2,64,512]{3,2,1,0:T(8,128)(2,1)S(1)} %bitcast.3, f32[32,128]{1,0:T(8,128)S(1)} %bitcast.4, s32[1,512]{1,0:T(1,128)S(1)} %bitcast.5, s32[6,12]{1,0:T(8,128)S(1)} %copy-done.2), custom_call_target="tpu_custom_call" | custom-call | flops 1711276032 | bytes 4194304 | tf_op jit(solution)/shard_map/density_blocks/pallas_call | solution.py:252
  57.0 0.8 %copy.6 = bf16[6,3,128,128]{3,2,1,0:T(8,128)(2,1)} copy(bf16[6,3,128,128]{3,2,1,0:T(8,128)(2,1)S(1)} %density_blocks.1) | data formatting | bytes 1179648
Async XLA Ops:
  0.0 0.7 %copy-start.2 = (s32[6,12]{1,0:T(8,128)S(1)}, s32[6,12]{1,0:T(8,128)}, u32[]{:S(2)}) copy-start(s32[6,12]{1,0:T(8,128)} %pattern.1) | copy-start | bytes 868
  0.7 1.1 %copy-start = (bf16[768,512]{1,0:T(8,128)(2,1)S(1)}, bf16[768,512]{1,0:T(8,128)(2,1)}, u32[]{:S(2)}) copy-start(bf16[768,512]{1,0:T(8,128)(2,1)} %param.4) | copy-start | bytes 2359300
  1.8 0.7 %copy-start.1 = (f32[4096]{0:T(1024)S(1)}, f32[4096]{0:T(1024)}, u32[]{:S(2)}) copy-start(f32[4096]{0:T(1024)} %param.5) | copy-start | bytes 49156
  2.5 0.7 %copy-start.3 = (s32[512]{0:T(512)S(1)}, s32[512]{0:T(512)}, u32[]{:S(2)}) copy-start(s32[512]{0:T(512)} %param.6) | copy-start | bytes 6148

commit v2 on v1

v2 whole, which is shorter than its diff:
```python
import functools

import jax
import jax.numpy as jnp
from jax import lax
from jax.experimental import pallas as pl
from jax.experimental.pallas import tpu as pltpu
from jax.sharding import PartitionSpec as P

MESH = pl.DeviceIdType.MESH
B = 128
REACH = 8
BAND = 2 * REACH + 1
OWN = 6
WINDOW = OWN + 2 * REACH
NJ = 2
JC = B // NJ
HALF = JC // 2
JOBS = OWN * NJ
SHARE = 3
LAG = 5
FAR_AT = NJ


def kernel(
    n_clusters, slab, occ, band, pattern, out,
    window, scaled, blocks, kept, up_out, up_in, down_out, down_in, total, result,
    occ_v, band_v, pat,
    own_sem, in_sem, near_send, near_recv, core_send, core_recv, far_send, far_recv,
    relay_send, relay_recv, up_send, up_recv, down_send, down_recv, out_sem, hello,
):
    wide = lax.axis_index("wide")
    here = lax.axis_index("narrow")
    n_chips = lax.axis_size("wide") // 2
    n_narrow = lax.axis_size("narrow")
    chip, core = wide // 2, lax.rem(wide, 2)
    outward = 2 * core - 1
    near_chip = lax.rem(chip + outward + n_chips, n_chips)
    far_chip = lax.rem(chip - outward + n_chips, n_chips)
    other = (chip * 2 + 1 - core, here)
    near_other = (near_chip * 2 + 1 - core, here)
    near_same = (near_chip * 2 + core, here)
    far_same = (far_chip * 2 + core, here)
    up = (wide, lax.rem(here + 1, n_narrow))
    down = (wide, lax.rem(here + n_narrow - 1, n_narrow))
    first_0 = jnp.logical_and(chip == 0, core == 0)
    first_1 = jnp.logical_and(chip == 0, core == 1)
    last_1 = jnp.logical_and(chip == n_chips - 1, core == 1)
    far_early = jnp.logical_and(core == 0, jnp.logical_or(chip == 0, chip == n_chips - 1))

    def by_core(zero, one):
        return jnp.where(core == 0, zero, one)

    own = [
        pltpu.make_async_copy(slab.at[:, h], window.at[h, pl.ds(REACH, OWN)], own_sem.at[h])
        for h in range(NJ)
    ]
    small = [
        pltpu.make_async_copy(occ, occ_v, in_sem.at[0]),
        pltpu.make_async_copy(band, band_v, in_sem.at[1]),
        pltpu.make_async_copy(pattern, pat, in_sem.at[2]),
    ]
    for copy in own + small:
        copy.start()

    def signal(sem, device):
        pl.semaphore_signal(sem, inc=1, device_id=device, device_id_type=MESH)

    barrier = pltpu.get_barrier_semaphore()
    signal(barrier, up)
    signal(barrier, down)

    @pl.when(jnp.logical_not(first_0))
    def _():
        signal(barrier, other)

    @pl.when(jnp.logical_not(last_1))
    def _():
        signal(barrier, near_other)
        signal(barrier, near_same)

    @pl.when(first_1)
    def _():
        signal(barrier, far_same)

    pl.semaphore_wait(
        barrier,
        5 - first_0.astype(jnp.int32) - 2 * first_1.astype(jnp.int32) + last_1.astype(jnp.int32),
    )

    @pl.when(first_0)
    def _():
        signal(hello.at[1], other)

    @pl.when(last_1)
    def _():
        signal(hello.at[0], near_other)
        signal(hello.at[0], near_same)

    def remote(src, dst, send_sem, recv_sem, device):
        return pltpu.make_async_remote_copy(
            src_ref=src, dst_ref=dst, send_sem=send_sem, recv_sem=recv_sem,
            device_id=device, device_id_type=MESH,
        )

    def near_copy(h, i):
        n = 2 if i == 0 else 1
        src = by_core(0, 4) if i == 0 else by_core(i + 1, 4 - i)
        dst = by_core(14, 6) if i == 0 else by_core(15 + i, 6 - i)
        return remote(
            slab.at[pl.ds(src, n), h], window.at[h, pl.ds(dst, n)],
            near_send.at[h, i], near_recv.at[h, i], near_other,
        )

    def near_arrived(h, i):
        n = 2 if i == 0 else 1
        at = by_core(6, 14) if i == 0 else by_core(6 - i, 15 + i)
        there = window.at[h, pl.ds(at, n)]
        remote(there, there, near_send.at[h, i], near_recv.at[h, i], near_other).wait_recv()

    def core_copy(h):
        return remote(
            slab.at[:, h], window.at[h, pl.ds(by_core(2, 14), OWN)],
            core_send.at[h], core_recv.at[h], other,
        )

    def core_arrived(h):
        there = window.at[h, pl.ds(by_core(14, 2), OWN)]
        remote(there, there, core_send.at[h], core_recv.at[h], other).wait_recv()

    def far_copy(h):
        return remote(
            slab.at[pl.ds(by_core(4, 0), 2), h], window.at[h, pl.ds(by_core(0, 20), 2)],
            far_send.at[h], far_recv.at[h], far_same,
        )

    def far_arrived(h):
        there = window.at[h, pl.ds(by_core(0, 20), 2)]
        remote(there, there, far_send.at[h], far_recv.at[h], far_same).wait_recv()

    def relay_copy(h):
        return remote(
            window.at[h, pl.ds(by_core(6, 14), 2)], window.at[h, pl.ds(by_core(0, 20), 2)],
            relay_send.at[h], relay_recv.at[h], other,
        )

    def relay_arrived(h):
        there = window.at[h, pl.ds(by_core(20, 0), 2)]
        remote(there, there, relay_send.at[h], relay_recv.at[h], other).wait_recv()

    def all_near():
        for h in range(NJ):
            for i in range(2):
                near_copy(h, i).start()
        for i in range(2, 5):
            for h in range(NJ):
                near_copy(h, i).start()

    def all_far():
        for h in range(NJ):
            far_copy(h).start()

    with jax.named_scope("first_sends"):
        pl.when(jnp.logical_not(first_0))(all_near)
        pl.when(far_early)(all_far)

        @pl.when(first_1)
        def _():
            pl.semaphore_wait(hello.at[1], 1)

        for h in range(NJ):
            core_copy(h).start()

    with jax.named_scope("weights"):
        for copy in small:
            copy.wait()
        table = occ_v[...]
        turned = jnp.transpose(
            jnp.concatenate([table, jnp.zeros((B - table.shape[0], B), jnp.float32)], axis=0)
        )
        bands = band_v[...]
        high, low = bands // B, lax.rem(bands, B)
        at = lax.broadcasted_iota(jnp.int32, (B, bands.shape[1]), 0)
        pick_high = jnp.where(at == high, 1.0, 0.0).astype(jnp.bfloat16)
        rest, found = turned, []
        for _ in range(3):
            piece = rest.astype(jnp.bfloat16)
            rest = rest - piece.astype(jnp.float32)
            found.append(jnp.dot(piece, pick_high, preferred_element_type=jnp.float32))
        looked = (found[2] + found[1]) + found[0]
        weight = jnp.sum(jnp.where(at == low, looked, 0.0), axis=0, keepdims=True)

    with jax.named_scope("scale"):
        for h in range(NJ):
            own[h].wait()
        for c in range(OWN):
            for h in range(NJ):
                rows = window[h, REACH + c].astype(jnp.float32) * weight
                scaled[c, pl.ds(h * JC, JC)] = rows.astype(jnp.bfloat16)

    @pl.when(first_0)
    def _():
        pl.semaphore_wait(hello.at[0], 1)
        all_near()

    def cluster(s):
        return jnp.where(first_1, 2 + s if s < 4 else 5 - s, by_core(OWN - 1 - s, s))

    def wait_rows(s, h):
        if s == 0:
            near_arrived(h, 0)
            relay_copy(h).start()
            near_arrived(h, 1)
            core_arrived(h)

        @pl.when(first_1)
        def _():
            if s == 0:
                near_arrived(h, 2)
                near_arrived(h, 3)
            elif s == 1:
                near_arrived(h, 4)
            elif s == 2:
                far_arrived(h)
            elif s == 4:
                relay_arrived(h)

        @pl.when(jnp.logical_not(first_1))
        def _():
            if s == 0:
                relay_arrived(h)
            elif s <= 3:
                near_arrived(h, s + 1)
            elif s == 4:
                far_arrived(h)

    def compute(job):
        s, h = divmod(job, NJ)
        c = cluster(s)
        right = window[h, pl.ds(c, BAND)].reshape(BAND * JC, -1)
        product = lax.dot_general(
            right, scaled[c], (((1,), (1,)), ((), ())), preferred_element_type=jnp.float32
        )
        blocks[...] = product.astype(jnp.bfloat16).reshape(BAND, JC, B)
        mine = wide * OWN + c
        for r in (2, 1, 3, 0):
            for m in range(SHARE):
                slot = lax.rem(here + r, n_narrow) * SHARE + m
                entry = pat[c, slot] - mine + REACH
                entry = jnp.where(entry < 0, entry + n_clusters, entry)
                entry = jnp.where(entry >= n_clusters, entry - n_clusters, entry)
                block = blocks[jnp.clip(entry, 0, BAND - 1)]
                one, two = block[:HALF], block[HALF:]
                if r == 2:
                    up_out[job, 0, m] = one
                    down_out[job, 0, m] = two
                elif r == 1:
                    up_out[job + LAG, 1, m] = one
                    up_out[job + LAG, 2, m] = two
                elif r == 3:
                    down_out[job + LAG, 2, m] = one
                    down_out[job + LAG, 1, m] = two
                else:
                    kept[job, 0, m] = one
                    kept[job, 1, m] = two

    def message(t, src, dst, send_sem, recv_sem, device):
        first, last = (0 if t < JOBS else 1), (3 if t >= LAG else 1)
        part = pl.ds(first, last - first)
        return remote(src.at[t, part], dst.at[t, part], send_sem.at[t], recv_sem.at[t], device)

    def up_message(t):
        return message(t, up_out, up_in, up_send, up_recv, up)

    def down_message(t):
        return message(t, down_out, down_in, down_send, down_recv, down)

    def add_first(t):
        for src, dst in ((up_in, up_out), (down_in, down_out)):
            dst[t, 1] = (
                dst[t, 1].astype(jnp.float32) + src[t - LAG, 0].astype(jnp.float32)
            ).astype(jnp.bfloat16)

    def finish(t):
        job = t - LAG
        s, h = divmod(job, NJ)
        c = cluster(s)
        for half in range(2):
            total[:, pl.ds(h * JC + half * HALF, HALF)] = (
                kept[job, half].astype(jnp.float32)
                + up_in[t, 1 + half].astype(jnp.float32)
                + down_in[t, 2 - half].astype(jnp.float32)
            )
        if h == NJ - 1:
            for m in range(SHARE):
                result[c, m] = jnp.transpose(total[m]).astype(jnp.bfloat16)
            pltpu.make_async_copy(result.at[c], out.at[c], out_sem.at[s]).start()

    for t in range(JOBS + 2 * LAG):
        if t < JOBS:
            with jax.named_scope("wait_rows"):
                wait_rows(*divmod(t, NJ))
            with jax.named_scope("blocks"):
                compute(t)
        if t >= LAG:
            with jax.named_scope("wait_parts"):
                up_message(t - LAG).wait_recv()
                down_message(t - LAG).wait_recv()
        if t < JOBS + LAG:
            with jax.named_scope("send_parts"):
                if t >= LAG:
                    add_first(t)
                up_message(t).start()
                down_message(t).start()
        if t == FAR_AT:

            @pl.when(first_1)
            def _():
                pl.semaphore_wait(hello.at[0], 1)

            pl.when(jnp.logical_not(far_early))(all_far)
        if t >= 2 * LAG:
            with jax.named_scope("finish"):
                finish(t - LAG)

    with jax.named_scope("drain"):
        for h in range(NJ):
            for i in range(5):
                near_copy(h, i).wait_send()
            core_copy(h).wait_send()
            far_copy(h).wait_send()
            relay_copy(h).wait_send()
        for t in range(JOBS + LAG):
            up_message(t).wait_send()
            down_message(t).wait_send()
        for s in range(OWN):
            c = cluster(s)
            pltpu.make_async_copy(result.at[c], out.at[c], out_sem.at[s]).wait()


def per_device(slab, occupation, column_band, pattern):
    cols = slab.shape[1]
    n_clusters = OWN * lax.axis_size("wide")
    dma = pltpu.SemaphoreType.DMA
    bf16, f32 = jnp.bfloat16, jnp.float32
    return pl.pallas_call(
        functools.partial(kernel, n_clusters),
        out_shape=jax.ShapeDtypeStruct((OWN, SHARE, B, B), bf16),
        in_specs=[pl.BlockSpec(memory_space=pl.ANY)] * 4,
        out_specs=pl.BlockSpec(memory_space=pl.ANY),
        scratch_shapes=[
            pltpu.VMEM((NJ, WINDOW, JC, cols), bf16),
            pltpu.VMEM((OWN, B, cols), bf16),
            pltpu.VMEM((BAND, JC, B), bf16),
            pltpu.VMEM((JOBS, 2, SHARE, HALF, B), bf16),
            *[pltpu.VMEM((JOBS + LAG, 3, SHARE, HALF, B), bf16)] * 4,
            pltpu.VMEM((SHARE, B, B), f32),
            pltpu.VMEM((OWN, SHARE, B, B), bf16),
            pltpu.VMEM((occupation.shape[0] // B, B), f32),
            pltpu.VMEM((1, cols), jnp.int32),
            pltpu.SMEM(pattern.shape, jnp.int32),
            dma((NJ,)), dma((3,)), dma((NJ, 5)), dma((NJ, 5)),
            *[dma((NJ,))] * 6,
            *[dma((JOBS + LAG,))] * 4,
            dma((OWN,)), pltpu.SemaphoreType.REGULAR((2,)),
        ],
        compiler_params=pltpu.CompilerParams(
            collective_id=0, has_side_effects=True, vmem_limit_bytes=60 * 2**20
        ),
        cost_estimate=pl.CostEstimate(
            flops=2 * OWN * BAND * B * B * cols, bytes_accessed=4 * 2**20, transcendentals=0
        ),
        name="density_blocks",
    )(
        slab.reshape(OWN, NJ, JC, cols),
        occupation.reshape(-1, B),
        column_band.reshape(1, -1),
        pattern,
    )


def solution(mesh):
    placed = (P("wide", "narrow"), P(), P("narrow"), P("wide", None))
    return jax.shard_map(
        per_device,
        mesh=mesh,
        in_specs=placed,
        out_specs=P("wide", "narrow", None, None),
        check_vma=False,
    )
```

time: 58.1 us -> 44.8 us (0.77)
  Pallas kernels: 53.8 us -> 42.6 us
  local copies, waits for them, and re-layouts: 4.03 us -> 1.93 us
    pallas_call x1, Pallas kernels: 53.8 us -> 42.6 us  [per_device(): pl.pallas_call(functools.partial(kernel, n_clusters), out_shape=jax.Shape...]
    unnamed x9 -> x1, local copies, waits for them, and re-layouts: 4.03 us -> 1.93 us
where the time goes in v2:
time: 44.8 us; the launch traced here: 44.6 us
  Pallas kernels  42.6 us (95%)
  local copies, waits for them, and re-layouts  1.93 us (4%)
    pallas_call x1, Pallas kernels, per_device(): pl.pallas_call(functools.partial(kernel, n_clusters), out_shape=jax.Shape...  42.6 us
    unnamed x1, local copies, waits for them, and re-layouts  1.93 us

profile of v2, /device:TPU:2, one launch (start us, length us, event | category | flops | bytes accessed | tf_op | source)
XLA Modules:
  0.0 44.6 jit_solution(17186712447411225250)
XLA Ops:
  0.0 42.6 %density_blocks.1 = bf16[6,3,128,128]{3,2,1,0:T(8,128)(2,1)} custom-call(bf16[6,2,64,512]{3,2,1,0:T(8,128)(2,1)} %bitcast.3, f32[32,128]{1,0:T(8,128)} %bitcast.4, s32[1,512]{1,0:T(1,128)} %bitcast.5, s32[6,12]{1,0:T(8,128)} %pattern.1), custom_call_target="tpu_custom_call" | custom-call | flops 1711276032 | bytes 4194304 | tf_op jit(solution)/shard_map/density_blocks/pallas_call | solution.py:346
  42.7 1.9 %copy.6 = bf16[6,3,128,128]{3,2,1,0:T(8,128)(2,1)} copy(bf16[6,3,128,128]{3,2,1,0:T(8,128)(2,1)} %density_blocks.1) | data formatting | bytes 1179648

commit v3 on v2

--- a/solution.py
+++ b/solution.py
@@ -19,7 +19,6 @@
 JOBS = OWN * NJ
 SHARE = 3
 LAG = 5
-FAR_AT = NJ
 
 
 def kernel(
@@ -36,17 +35,13 @@
     chip, core = wide // 2, lax.rem(wide, 2)
     outward = 2 * core - 1
     near_chip = lax.rem(chip + outward + n_chips, n_chips)
-    far_chip = lax.rem(chip - outward + n_chips, n_chips)
     other = (chip * 2 + 1 - core, here)
     near_other = (near_chip * 2 + 1 - core, here)
-    near_same = (near_chip * 2 + core, here)
-    far_same = (far_chip * 2 + core, here)
     up = (wide, lax.rem(here + 1, n_narrow))
     down = (wide, lax.rem(here + n_narrow - 1, n_narrow))
     first_0 = jnp.logical_and(chip == 0, core == 0)
     first_1 = jnp.logical_and(chip == 0, core == 1)
     last_1 = jnp.logical_and(chip == n_chips - 1, core == 1)
-    far_early = jnp.logical_and(core == 0, jnp.logical_or(chip == 0, chip == n_chips - 1))
 
     def by_core(zero, one):
         return jnp.where(core == 0, zero, one)
@@ -77,16 +72,8 @@
     @pl.when(jnp.logical_not(last_1))
     def _():
         signal(barrier, near_other)
-        signal(barrier, near_same)
-
-    @pl.when(first_1)
-    def _():
-        signal(barrier, far_same)
-
-    pl.semaphore_wait(
-        barrier,
-        5 - first_0.astype(jnp.int32) - 2 * first_1.astype(jnp.int32) + last_1.astype(jnp.int32),
-    )
+
+    pl.semaphore_wait(barrier, 4 - (chip == 0).astype(jnp.int32))
 
     @pl.when(first_0)
     def _():
@@ -95,7 +82,6 @@
     @pl.when(last_1)
     def _():
         signal(hello.at[0], near_other)
-        signal(hello.at[0], near_same)
 
     def remote(src, dst, send_sem, recv_sem, device):
         return pltpu.make_async_remote_copy(
@@ -130,13 +116,13 @@
 
     def far_copy(h):
         return remote(
-            slab.at[pl.ds(by_core(4, 0), 2), h], window.at[h, pl.ds(by_core(0, 20), 2)],
-            far_send.at[h], far_recv.at[h], far_same,
+            window.at[h, pl.ds(by_core(14, 6), 2)], window.at[h, pl.ds(by_core(20, 0), 2)],
+            far_send.at[h], far_recv.at[h], near_other,
         )
 
     def far_arrived(h):
         there = window.at[h, pl.ds(by_core(0, 20), 2)]
-        remote(there, there, far_send.at[h], far_recv.at[h], far_same).wait_recv()
+        remote(there, there, far_send.at[h], far_recv.at[h], near_other).wait_recv()
 
     def relay_copy(h):
         return remote(
@@ -156,13 +142,8 @@
             for h in range(NJ):
                 near_copy(h, i).start()
 
-    def all_far():
-        for h in range(NJ):
-            far_copy(h).start()
-
     with jax.named_scope("first_sends"):
         pl.when(jnp.logical_not(first_0))(all_near)
-        pl.when(far_early)(all_far)
 
         @pl.when(first_1)
         def _():
@@ -210,8 +191,9 @@
         if s == 0:
             near_arrived(h, 0)
             relay_copy(h).start()
+            core_arrived(h)
+            far_copy(h).start()
             near_arrived(h, 1)
-            core_arrived(h)
 
         @pl.when(first_1)
         def _():
@@ -312,13 +294,6 @@
                     add_first(t)
                 up_message(t).start()
                 down_message(t).start()
-        if t == FAR_AT:
-
-            @pl.when(first_1)
-            def _():
-                pl.semaphore_wait(hello.at[0], 1)
-
-            pl.when(jnp.logical_not(far_early))(all_far)
         if t >= 2 * LAG:
             with jax.named_scope("finish"):
                 finish(t - LAG)

time: 44.8 us -> 42.4 us (0.946)
  the two profiles are of different devices: /device:TPU:2 before, /device:TPU:4 now
where the time goes in v3:
time: 42.4 us; the launch traced here: 42.2 us
  Pallas kernels  40.3 us (95%)
  local copies, waits for them, and re-layouts  1.93 us (5%)
    pallas_call x1, Pallas kernels, per_device(): pl.pallas_call(functools.partial(kernel, n_clusters), out_shape=jax.Shape...  40.3 us
    unnamed x1, local copies, waits for them, and re-layouts  1.93 us

profile of v3, /device:TPU:4, one launch (start us, length us, event | category | flops | bytes accessed | tf_op | source)
XLA Modules:
  0.0 42.2 jit_solution(11090811305191809183)
XLA Ops:
  0.0 40.3 %density_blocks.1 = bf16[6,3,128,128]{3,2,1,0:T(8,128)(2,1)} custom-call(bf16[6,2,64,512]{3,2,1,0:T(8,128)(2,1)} %bitcast.3, f32[32,128]{1,0:T(8,128)} %bitcast.4, s32[1,512]{1,0:T(1,128)} %bitcast.5, s32[6,12]{1,0:T(8,128)} %pattern.1), custom_call_target="tpu_custom_call" | custom-call | flops 1711276032 | bytes 4194304 | tf_op jit(solution)/shard_map/density_blocks/pallas_call | solution.py:321
  40.3 1.9 %copy.6 = bf16[6,3,128,128]{3,2,1,0:T(8,128)(2,1)} copy(bf16[6,3,128,128]{3,2,1,0:T(8,128)(2,1)} %density_blocks.1) | data formatting | bytes 1179648

commit v4 on v3

--- a/solution.py
+++ b/solution.py
@@ -18,7 +18,9 @@
 HALF = JC // 2
 JOBS = OWN * NJ
 SHARE = 3
-LAG = 5
+STRAIGHT = 8
+LAG = 6
+AHEAD = (0, 0, 0, 2, 1, 1, 0, 1, 1, 1, 1, 1)
 
 
 def kernel(
@@ -26,7 +28,8 @@
     window, scaled, blocks, kept, up_out, up_in, down_out, down_in, total, result,
     occ_v, band_v, pat,
     own_sem, in_sem, near_send, near_recv, core_send, core_recv, far_send, far_recv,
-    relay_send, relay_recv, up_send, up_recv, down_send, down_recv, out_sem, hello,
+    relay_send, relay_recv, up_send, up_recv, down_send, down_recv,
+    up2_send, up2_recv, down2_send, down2_recv, out_sem, hello,
 ):
     wide = lax.axis_index("wide")
     here = lax.axis_index("narrow")
@@ -39,6 +42,7 @@
     near_other = (near_chip * 2 + 1 - core, here)
     up = (wide, lax.rem(here + 1, n_narrow))
     down = (wide, lax.rem(here + n_narrow - 1, n_narrow))
+    across = (wide, lax.rem(here + 2, n_narrow))
     first_0 = jnp.logical_and(chip == 0, core == 0)
     first_1 = jnp.logical_and(chip == 0, core == 1)
     last_1 = jnp.logical_and(chip == n_chips - 1, core == 1)
@@ -73,7 +77,11 @@
     def _():
         signal(barrier, near_other)
 
-    pl.semaphore_wait(barrier, 4 - (chip == 0).astype(jnp.int32))
+    @pl.when(first_1)
+    def _():
+        signal(barrier, across)
+
+    pl.semaphore_wait(barrier, 4 - first_0.astype(jnp.int32))
 
     @pl.when(first_0)
     def _():
@@ -184,19 +192,16 @@
         pl.semaphore_wait(hello.at[0], 1)
         all_near()
 
-    def cluster(s):
-        return jnp.where(first_1, 2 + s if s < 4 else 5 - s, by_core(OWN - 1 - s, s))
-
-    def wait_rows(s, h):
+    for h in range(NJ):
+        core_arrived(h)
+        far_copy(h).start()
+
+    def wait_rows(s, h, inner_last):
         if s == 0:
             near_arrived(h, 0)
             relay_copy(h).start()
-            core_arrived(h)
-            far_copy(h).start()
             near_arrived(h, 1)
-
-        @pl.when(first_1)
-        def _():
+        if inner_last:
             if s == 0:
                 near_arrived(h, 2)
                 near_arrived(h, 3)
@@ -206,17 +211,14 @@
                 far_arrived(h)
             elif s == 4:
                 relay_arrived(h)
-
-        @pl.when(jnp.logical_not(first_1))
-        def _():
-            if s == 0:
-                relay_arrived(h)
-            elif s <= 3:
-                near_arrived(h, s + 1)
-            elif s == 4:
-                far_arrived(h)
-
-    def compute(job):
+        elif s == 0:
+            relay_arrived(h)
+        elif s <= 3:
+            near_arrived(h, s + 1)
+        elif s == 4:
+            far_arrived(h)
+
+    def compute(job, cluster):
         s, h = divmod(job, NJ)
         c = cluster(s)
         right = window[h, pl.ds(c, BAND)].reshape(BAND * JC, -1)
@@ -263,40 +265,128 @@
                 dst[t, 1].astype(jnp.float32) + src[t - LAG, 0].astype(jnp.float32)
             ).astype(jnp.bfloat16)
 
-    def finish(t):
+    def finish(t, cluster, direct=False):
         job = t - LAG
         s, h = divmod(job, NJ)
         c = cluster(s)
         for half in range(2):
-            total[:, pl.ds(h * JC + half * HALF, HALF)] = (
+            value = (
                 kept[job, half].astype(jnp.float32)
                 + up_in[t, 1 + half].astype(jnp.float32)
                 + down_in[t, 2 - half].astype(jnp.float32)
             )
+            if direct:
+                value += (up_in if half == 0 else down_in)[job, 0].astype(jnp.float32)
+            total[:, pl.ds(h * JC + half * HALF, HALF)] = value
         if h == NJ - 1:
             for m in range(SHARE):
                 result[c, m] = jnp.transpose(total[m]).astype(jnp.bfloat16)
             pltpu.make_async_copy(result.at[c], out.at[c], out_sem.at[s]).start()
 
-    for t in range(JOBS + 2 * LAG):
-        if t < JOBS:
-            with jax.named_scope("wait_rows"):
-                wait_rows(*divmod(t, NJ))
-            with jax.named_scope("blocks"):
-                compute(t)
-        if t >= LAG:
-            with jax.named_scope("wait_parts"):
+    def results_written(cluster):
+        for s in range(OWN):
+            c = cluster(s)
+            pltpu.make_async_copy(result.at[c], out.at[c], out_sem.at[s]).wait()
+
+    def outwards():
+        def cluster(s):
+            return by_core(OWN - 1 - s, s)
+
+        for t in range(JOBS + 2 * LAG):
+            if t < JOBS:
+                wait_rows(*divmod(t, NJ), False)
+                compute(t, cluster)
+            if t >= LAG:
                 up_message(t - LAG).wait_recv()
                 down_message(t - LAG).wait_recv()
-        if t < JOBS + LAG:
-            with jax.named_scope("send_parts"):
+            if t < JOBS + LAG:
                 if t >= LAG:
                     add_first(t)
                 up_message(t).start()
                 down_message(t).start()
-        if t >= 2 * LAG:
-            with jax.named_scope("finish"):
-                finish(t - LAG)
+            if t >= 2 * LAG:
+                finish(t - LAG, cluster)
+        for t in range(JOBS + LAG):
+            up_message(t).wait_send()
+            down_message(t).wait_send()
+        results_written(cluster)
+
+    def outer_first():
+        def cluster(s):
+            return 2 + s if s < 4 else 5 - s
+
+        def pair(t, first, n, send, recv):
+            part = pl.ds(first, n)
+            return (
+                remote(up_out.at[t, part], up_in.at[t, part], send[0], recv[0], up),
+                remote(down_out.at[t, part], down_in.at[t, part], send[1], recv[1], down),
+            )
+
+        def first_pair(job):
+            return pair(
+                job, 0, 1, (up_send.at[job], down_send.at[job]), (up_recv.at[job], down_recv.at[job])
+            )
+
+        def sum_pair(job):
+            return pair(
+                job + LAG, 1, 2,
+                (up2_send.at[job], down2_send.at[job]), (up2_recv.at[job], down2_recv.at[job]),
+            )
+
+        def straight(job):
+            part = pl.ds(1, 2)
+            t = job + LAG
+            return (
+                remote(up_out.at[job, 0], up_in.at[job, 0], up2_send.at[job], up2_recv.at[job], across),
+                remote(down_out.at[job, 0], down_in.at[job, 0], down2_send.at[job], down2_recv.at[job], across),
+                remote(up_out.at[t, part], up_in.at[t, part], up_send.at[job], up_recv.at[job], up),
+                remote(down_out.at[t, part], down_in.at[t, part], down_send.at[job], down_recv.at[job], down),
+            )
+
+        def started(job):
+            return straight(job) if job < STRAIGHT else first_pair(job)
+
+        def pass_on(job):
+            if job < STRAIGHT:
+                return
+            for copy in first_pair(job):
+                copy.wait_recv()
+            add_first(job + LAG)
+            for copy in sum_pair(job):
+                copy.start()
+
+        def end(job):
+            for copy in straight(job) if job < STRAIGHT else sum_pair(job):
+                copy.wait_recv()
+            finish(job + LAG, cluster, job < STRAIGHT)
+
+        passed = ended = 0
+        for t in range(JOBS):
+            wait_rows(*divmod(t, NJ), True)
+            compute(t, cluster)
+            for copy in started(t):
+                copy.start()
+            for _ in range(AHEAD[t]):
+                pass_on(passed)
+                passed += 1
+            if passed - ended > 5:
+                end(ended)
+                ended += 1
+        while passed < JOBS:
+            pass_on(passed)
+            passed += 1
+            if passed - ended > 5:
+                end(ended)
+                ended += 1
+        for job in range(ended, JOBS):
+            end(job)
+        for job in range(JOBS):
+            for copy in started(job) + (() if job < STRAIGHT else sum_pair(job)):
+                copy.wait_send()
+        results_written(cluster)
+
+    pl.when(first_1)(outer_first)
+    pl.when(jnp.logical_not(first_1))(outwards)
 
     with jax.named_scope("drain"):
         for h in range(NJ):
@@ -305,12 +395,6 @@
             core_copy(h).wait_send()
             far_copy(h).wait_send()
             relay_copy(h).wait_send()
-        for t in range(JOBS + LAG):
-            up_message(t).wait_send()
-            down_message(t).wait_send()
-        for s in range(OWN):
-            c = cluster(s)
-            pltpu.make_async_copy(result.at[c], out.at[c], out_sem.at[s]).wait()
 
 
 def per_device(slab, occupation, column_band, pattern):
@@ -337,6 +421,7 @@
             dma((NJ,)), dma((3,)), dma((NJ, 5)), dma((NJ, 5)),
             *[dma((NJ,))] * 6,
             *[dma((JOBS + LAG,))] * 4,
+            *[dma((JOBS,))] * 4,
             dma((OWN,)), pltpu.SemaphoreType.REGULAR((2,)),
         ],
         compiler_params=pltpu.CompilerParams(

time: 42.4 us -> 41.1 us (0.969)
  the two profiles are of different devices: /device:TPU:4 before, /device:TPU:2 now
where the time goes in v4:
time: 41.1 us; the launch traced here: 41 us
  Pallas kernels  39 us (95%)
  local copies, waits for them, and re-layouts  1.93 us (5%)
    pallas_call x1, Pallas kernels, per_device(): pl.pallas_call(functools.partial(kernel, n_clusters), out_shape=jax.Shape...  39 us
    unnamed x1, local copies, waits for them, and re-layouts  1.93 us

profile of v4, /device:TPU:2, one launch (start us, length us, event | category | flops | bytes accessed | tf_op | source)
XLA Modules:
  0.0 41.0 jit_solution(6662597172430386155)
XLA Ops:
  0.0 39.0 %density_blocks.1 = bf16[6,3,128,128]{3,2,1,0:T(8,128)(2,1)} custom-call(bf16[6,2,64,512]{3,2,1,0:T(8,128)(2,1)} %bitcast.3, f32[32,128]{1,0:T(8,128)} %bitcast.4, s32[1,512]{1,0:T(1,128)} %bitcast.5, s32[6,12]{1,0:T(8,128)} %pattern.1), custom_call_target="tpu_custom_call" | custom-call | flops 1711276032 | bytes 4194304 | tf_op jit(solution)/shard_map/density_blocks/pallas_call | solution.py:405
  39.0 1.9 %copy.6 = bf16[6,3,128,128]{3,2,1,0:T(8,128)(2,1)} copy(bf16[6,3,128,128]{3,2,1,0:T(8,128)(2,1)} %density_blocks.1) | data formatting | bytes 1179648
